TPU v7x, 128 devices: a whole 4x4x4 slice. The times are simulated.
128 devices in a mesh: region: 8 (over z, core), block: 16 (over y, x).
Axes of the slice: x: 4, y: 4, z: 4, core: 2. Of those that a mesh axis runs over, the one named last changes fastest.
Arguments:
- point_feats: bfloat16 [393216, 64], P(('region', 'block')), may hold values from -6 to 6
- point_block: int32 [393216, 1], P(('region', 'block')), may hold values from 0 to 15; in each aligned block of 3072 rows (0 to 3071, 3072 to 6143, ...) at most 384 rows name the same one
- point_voxel: int32 [393216], P(('region', 'block')), may hold values from 0 to 4095
- neighbours: int32 [128, 6], P(('region', 'block')), may hold values from -1 to 127, as said below
- conv_one: bfloat16 [27, 64, 64], replicated, may hold values from -0.15625 to 0.15625
- bias_one: float32 [64], replicated, may hold values from -3 to 3
- conv_two: bfloat16 [27, 64, 64], replicated, may hold values from -0.15625 to 0.15625
- bias_two: float32 [64], replicated, may hold values from -3 to 3
Outputs:
- encoded: bfloat16 [128, 16, 16, 16, 64], P(('region', 'block'))
Inputs may be any that keep to these rules, and one draw needn't show every extreme that they name: `point_block`: within the rows of one device no block is named by more than 384 points, and some block is named by exactly 384. `neighbours`: links are symmetric: if face f of block g names block h, face f xor 1 of h names g. Faces 2 to 5 name only blocks of the same device. Faces 0 and 1 name a block of the same device or one of the device with the same block index and region index one lower (face 0) or one higher (face 1); on each device exactly one block has face 1 naming a block on the next region (none on the last region), and exactly one has face 0 naming a block on the previous region (none on the first).
All inputs are finite; a program needn't handle non-finite values.
Results may differ from a plain program's by a relative error of at most 0.0045.
Values may be sent and summed in bfloat16 or wider, within the bound.
A program may use at most 128 MiB of HBM per device.

v0:
```python
import functools
import math

import jax
import jax.numpy as jnp
from jax import lax
from jax.experimental import pallas as pl
from jax.experimental.pallas import tpu as pltpu
from jax.sharding import PartitionSpec as P

BE = 16
C = 64
ROWS = BE * BE
ZG = 4
WIDE = 4 * C
ZPAD = (BE + 2) * C
TAP = 6 * C
NT = (((1,), (1,)), ((), ()))
F32 = jnp.float32
BF16 = jnp.bfloat16
MESH = pl.DeviceIdType.MESH


def iota(shape, dim):
    return lax.broadcasted_iota(jnp.int32, shape, dim)


def onehot(ids, row):
    return jnp.where(ids == row, jnp.ones((), BF16), jnp.zeros((), BF16))


def ranks_of(blk, columns):
    points = blk.shape[1]
    chunks = points // 256
    member = (iota((columns, points), 0) == blk).astype(F32)
    stacked = jnp.concatenate(
        [member[:, k * 256 : (k + 1) * 256] for k in range(chunks)], axis=0
    ).astype(BF16)
    before = (iota((256, 256), 0) < iota((256, 256), 1)).astype(F32).astype(BF16)
    prefix = jnp.dot(stacked, before, preferred_element_type=F32)
    totals = jnp.dot(stacked, jnp.ones((256, 256), BF16), preferred_element_type=F32)
    running = jnp.zeros((columns, 256), F32)
    rows = []
    for k in range(chunks):
        part = slice(k * columns, (k + 1) * columns)
        own = member[:, k * 256 : (k + 1) * 256]
        rows.append(jnp.sum(own * (prefix[part] + running), axis=0, keepdims=True))
        running = running + totals[part]
    return jnp.concatenate(rows, axis=1)


def build_weights(conv_ref, wide_ref):
    wide_ref[...] = jnp.zeros_like(wide_ref)

    def one(t, carry):
        w0, w1, w2 = conv_ref[3 * t], conv_ref[3 * t + 1], conv_ref[3 * t + 2]
        none = jnp.zeros_like(w0)
        pairs = ((w0, none), (w1, w0), (w2, w1), (none, w2))
        for k, pair in enumerate(pairs):
            tile = jnp.concatenate(pair, axis=1)
            for half in range(2):
                start = pl.multiple_of(t * TAP + (k + 2 * half) * C, C)
                wide_ref[pl.ds(start, C), half * 128 : (half + 1) * 128] = tile
        return carry

    lax.fori_loop(0, 9, one, 0)


def place_plane(field_ref, plane, groups, keep_y, keep_z):
    lane = iota((BE, 128), 1)
    rolled = []
    for group in groups:
        for half in range(2):
            rolled.append(pltpu.roll(group[:, half * 128 : (half + 1) * 128], 64, 1))
    before = [rolled[-1] * keep_z] + rolled
    after = rolled + [rolled[0] * keep_z]
    wide = jnp.concatenate(
        [jnp.where(lane < C, b, a) for b, a in zip(before, after)], axis=1
    )
    row, col = iota((BE, ZPAD), 0), iota((BE, ZPAD), 1)
    inner = ((col >= C) & (col < ZPAD - C)).astype(F32) * keep_y
    down = pltpu.roll(wide, 1, 0)
    down = jnp.where(row == 0, down * inner, down)
    up = pltpu.roll(wide, BE - 1, 0)
    up = jnp.where(row == BE - 1, up * inner, up)
    rows = pl.ds(pl.multiple_of(plane * BE, BE), BE)
    field_ref[0, rows, :] = down.astype(BF16)
    field_ref[1, rows, :] = wide.astype(BF16)
    field_ref[2, rows, :] = up.astype(BF16)


def convolve(field_ref, wide_ref, plane, count):
    def window(tap, group):
        dx, dy = divmod(tap, 3)
        start = (plane + dx) * BE
        return field_ref[dy, start : start + count * BE, group * WIDE : group * WIDE + TAP]

    total = None
    for first in range(0, 9, 2):
        taps = [t for t in (first, first + 1) if t < 9]
        left = jnp.concatenate(
            [
                jnp.concatenate([window(t, group) for t in taps], axis=1)
                for group in range(ZG)
            ],
            axis=0,
        )
        right = wide_ref[first * TAP : (first + len(taps)) * TAP, :]
        part = jnp.dot(left, right, preferred_element_type=F32)
        total = part if total is None else total + part
    return total


def body(
    dims, feats_ref, blk_ref, vox_ref, link_ref, one_ref, bone_ref, two_ref, btwo_ref, out_ref,
    expanded, indices, send, recv, sums, counts, inverse, voxels, field, wide_one, wide_two,
    side_out, side_in, send_sem, recv_sem, side_send, side_recv,
):
    regions, columns = dims
    side = math.isqrt(columns)
    points = blk_ref.shape[1]
    cap = 2 * points // columns
    quarter = cap // 4
    region, block = lax.axis_index("region"), lax.axis_index("block")
    my_y, my_x = block // side, block % side

    def at(dy, dx):
        return lax.rem(my_y + dy, side) * side + lax.rem(my_x + dx, side)

    barrier = pltpu.get_barrier_semaphore()
    for dy in range(side):
        for dx in range(side):
            if dy or dx:
                pl.semaphore_signal(
                    barrier, inc=1, device_id=(region, at(dy, dx)), device_id_type=MESH
                )

    @pl.when(region > 0)
    def _():
        pl.semaphore_signal(barrier, inc=1, device_id=(region - 1, block), device_id_type=MESH)

    @pl.when(region < regions - 1)
    def _():
        pl.semaphore_signal(barrier, inc=1, device_id=(region + 1, block), device_id_type=MESH)

    blk = blk_ref[...]
    rank = ranks_of(blk, columns)
    low = (
        (rank >= quarter).astype(F32)
        + (rank >= 2 * quarter).astype(F32)
        + (rank >= 3 * quarter).astype(F32)
    )
    high = rank - quarter * low
    feats = feats_ref[...]
    for k in range(4):
        expanded[k * C : (k + 1) * C, :] = feats * (low == k).astype(F32).astype(BF16)

    third = (rank >= 128).astype(F32) + (rank >= 256).astype(F32)
    place = (rank - 128 * third).astype(BF16)
    number = vox_ref[...]
    code_a = (number // 64 + 1).astype(F32).astype(BF16)
    code_b = (number % 64).astype(F32).astype(BF16)
    slot_row = (blk.astype(F32) * 16 + third).astype(BF16)
    where_to = onehot(iota((columns * 16, points), 0).astype(F32).astype(BF16), slot_row)
    spots = onehot(iota((128, points), 0).astype(F32).astype(BF16), place)
    codes = jnp.concatenate([spots * code_a, spots * code_b], axis=0)
    indices[...] = lax.dot_general(where_to, codes, NT, preferred_element_type=F32).astype(BF16)

    arrivals = columns - 1 + (region > 0).astype(jnp.int32) + (region < regions - 1).astype(jnp.int32)
    pl.semaphore_wait(barrier, arrivals)

    def copy_to(slot, target):
        return pltpu.make_async_remote_copy(
            src_ref=send.at[slot],
            dst_ref=recv.at[slot],
            send_sem=send_sem.at[slot],
            recv_sem=recv_sem.at[slot],
            device_id=(region, target),
            device_id_type=MESH,
        )

    def send_group(step, carry):
        turn = lax.rem(step + 1, side)
        targets = [at(j, lax.rem(turn + j, side)) for j in range(side)]
        blocks = blk_ref[...]
        placing = jnp.concatenate(
            [
                onehot(
                    iota((quarter, points), 0).astype(F32).astype(BF16),
                    jnp.where(blocks == target, high, -1.0).astype(BF16),
                )
                for target in targets
            ],
            axis=0,
        )
        packed = lax.dot_general(placing, expanded[...], NT, preferred_element_type=F32)
        packed = packed.astype(BF16)
        for j, target in enumerate(targets):
            slot = turn * side + j
            mine = packed[j * quarter : (j + 1) * quarter]
            codes_here = indices[pl.ds(pl.multiple_of(target * 16, 16), 16), :]

            def ship():
                send[slot, 0:quarter, :] = mine
                send[slot, quarter : quarter + 16, :] = codes_here
                copy_to(slot, target).start()

            if j == 0:

                @pl.when(turn == 0)
                def _():
                    recv[0, 0:quarter, :] = mine
                    recv[0, quarter : quarter + 16, :] = codes_here

                pl.when(turn != 0)(ship)
            else:
                ship()
        return carry

    lax.fori_loop(0, side, send_group, 0)

    build_weights(one_ref, wide_one)
    build_weights(two_ref, wide_two)

    sums[...] = jnp.zeros_like(sums)
    counts[...] = jnp.zeros_like(counts)

    def bin_group(step, carry):
        turn = lax.rem(step + 1, side)
        hots, masked, flat_hots, depth_hots = [], [], [], []
        for j in range(side):
            slot = turn * side + j
            if j == 0:
                pl.when(turn != 0)(lambda: copy_to(slot, block).wait_recv())
            else:
                copy_to(slot, block).wait_recv()
            code = recv[slot, quarter : quarter + 16, :].astype(F32)[0:8]
            a = code[:, 0:128].astype(jnp.int32) - 1
            b = code[:, 128:256].astype(jnp.int32)
            flat = a * 4 + (b >> 4)
            deep = (b >> 2) & 3
            inner = (b & 3).astype(F32)
            level = jnp.where(a >= 0, b & 15, -1).astype(F32)
            flat = flat.astype(F32)
            pieces = cap // 128
            ids = iota((ROWS, 128), 0).astype(F32).astype(BF16)
            by_group = []
            for group in range(ZG):
                row = jnp.where(deep == group, flat, -1.0)
                by_group.append(
                    jnp.concatenate(
                        [onehot(ids, row[k : k + 1].astype(BF16)) for k in range(pieces)], axis=1
                    )
                )
            hots.append(jnp.concatenate(by_group, axis=0))
            flat_hots.append(
                jnp.concatenate(
                    [onehot(ids, flat[k : k + 1].astype(BF16)) for k in range(pieces)], axis=1
                )
            )
            depth_hots.append(
                jnp.concatenate(
                    [onehot(ids[:BE], level[k : k + 1].astype(BF16)) for k in range(pieces)], axis=1
                )
            )
            turned = inner.T
            of_lane = (iota((128, WIDE), 1) // C).astype(F32)
            choose = jnp.concatenate(
                [(turned[:, k : k + 1] == of_lane).astype(F32) for k in range(pieces)], axis=0
            ).astype(BF16)
            quads = []
            for k in range(4):
                piece = recv[slot, 0:quarter, k * C : (k + 1) * C]
                quads.append(jnp.concatenate([piece] * 4, axis=1))
            masked.append(jnp.concatenate(quads, axis=0) * choose)
        hot = jnp.concatenate(hots, axis=1)
        sums[...] += jnp.dot(hot, jnp.concatenate(masked, axis=0), preferred_element_type=F32)
        counts[...] += lax.dot_general(
            jnp.concatenate(flat_hots, axis=1),
            jnp.concatenate(depth_hots, axis=1),
            NT,
            preferred_element_type=F32,
        )
        return carry

    lax.fori_loop(0, side, bin_group, 0)

    tally = counts[...]
    share = jnp.where(tally > 0.5, 1.0 / jnp.maximum(tally, 1.0), 0.0)
    first = share.astype(BF16)
    rest = share - first.astype(F32)
    second = rest.astype(BF16)
    third_part = (rest - second.astype(F32)).astype(BF16)
    spread = jnp.where(iota((BE, BE * C), 0) == iota((BE, BE * C), 1) // C, 1.0, 0.0).astype(BF16)
    inverse[...] = (
        jnp.dot(first, spread, preferred_element_type=F32)
        + jnp.dot(second, spread, preferred_element_type=F32)
        + jnp.dot(third_part, spread, preferred_element_type=F32)
    )

    keep_y = (link_ref[0, 2] >= 0).astype(F32)
    keep_z = (link_ref[0, 4] >= 0).astype(F32)

    def side_copy(layer, up):
        k = 2 * layer + up
        return pltpu.make_async_remote_copy(
            src_ref=side_out.at[k],
            dst_ref=side_in.at[k],
            send_sem=side_send.at[k],
            recv_sem=side_recv.at[k],
            device_id=(region + 1 if up else region - 1, block),
            device_id_type=MESH,
        )

    def send_sides(layer):
        pl.when(region > 0)(lambda: side_copy(layer, 0).start())
        pl.when(region < regions - 1)(lambda: side_copy(layer, 1).start())

    def receive_sides(layer):
        def put(k, plane):
            groups = [side_in[k, :, z * WIDE : (z + 1) * WIDE].astype(F32) for z in range(ZG)]
            place_plane(field.at[layer], plane, groups, 0.0, 0.0)

        def blank(plane):
            field[layer, :, plane * BE : (plane + 1) * BE, :] = jnp.zeros((3, BE, ZPAD), BF16)

        @pl.when(region > 0)
        def _():
            side_copy(layer, 1).wait_recv()
            put(2 * layer + 1, 0)

        @pl.when(region < regions - 1)
        def _():
            side_copy(layer, 0).wait_recv()
            put(2 * layer, BE + 1)

        pl.when(region == 0)(lambda: blank(0))
        pl.when(region == regions - 1)(lambda: blank(BE + 1))

    def settle_sides(layer):
        pl.when(region > 0)(lambda: side_copy(layer, 0).wait_send())
        pl.when(region < regions - 1)(lambda: side_copy(layer, 1).wait_send())

    def mean_plane(x):
        rows = pl.ds(pl.multiple_of(x * BE, BE), BE)
        groups = []
        for z in range(ZG):
            total = sums[pl.ds(pl.multiple_of(z * ROWS + x * BE, BE), BE), :]
            mean = (total * inverse[rows, z * WIDE : (z + 1) * WIDE]).astype(BF16)
            voxels[rows, z * WIDE : (z + 1) * WIDE] = mean
            groups.append(mean.astype(F32))
        place_plane(field.at[0], x + 1, groups, keep_y, keep_z)

    mean_plane(0)
    mean_plane(BE - 1)
    side_out[0] = voxels[0:BE, :]
    side_out[1] = voxels[ROWS - BE : ROWS, :]
    send_sides(0)
    lax.fori_loop(1, BE - 1, lambda x, carry: (mean_plane(x), carry)[1], 0)

    def encode(layer, plane, count, bias, save):
        total = convolve(field.at[layer], wide_one if layer == 0 else wide_two, plane, count)
        for x in range(count):
            rows = slice((plane + x) * BE, (plane + x + 1) * BE)
            groups = []
            for z in range(ZG):
                cols = slice(z * WIDE, (z + 1) * WIDE)
                start = z * count * BE + x * BE
                value = total[start : start + BE] + bias
                if layer:
                    value = value + voxels[rows, cols].astype(F32)
                value = jnp.where(inverse[rows, cols] > 0.0, jnp.maximum(value, 0.0), 0.0)
                groups.append(value)
            save(plane + x, groups)

    bias_one = jnp.concatenate([bone_ref[...]] * 4, axis=1)
    bias_two = jnp.concatenate([btwo_ref[...]] * 4, axis=1)

    def save_hidden(x, groups):
        groups = [g.astype(BF16) for g in groups]
        if x in (0, BE - 1):
            for z in range(ZG):
                side_out[2 if x == 0 else 3, :, z * WIDE : (z + 1) * WIDE] = groups[z]
        place_plane(field.at[1], x + 1, [g.astype(F32) for g in groups], keep_y, keep_z)

    def save_out(x, groups):
        for z in range(ZG):
            out_ref[x * BE : (x + 1) * BE, z * WIDE : (z + 1) * WIDE] = groups[z].astype(BF16)

    encode(0, 1, BE - 2, bias_one, save_hidden)
    receive_sides(0)
    encode(0, 0, 1, bias_one, save_hidden)
    encode(0, BE - 1, 1, bias_one, save_hidden)
    send_sides(1)
    encode(1, 1, BE - 2, bias_two, save_out)
    receive_sides(1)
    encode(1, 0, 1, bias_two, save_out)
    encode(1, BE - 1, 1, bias_two, save_out)

    def settle(slot, carry):
        copy_to(slot, block).wait_send()
        return carry

    lax.fori_loop(1, columns, settle, 0)
    settle_sides(0)
    settle_sides(1)


def per_device(
    dims, point_feats, point_block, point_voxel, neighbours, conv_one, bias_one, conv_two, bias_two
):
    regions, columns = dims
    points = point_feats.shape[0]
    quarter = 2 * points // columns // 4
    vmem = pl.BlockSpec(memory_space=pltpu.VMEM)
    smem = pl.BlockSpec(memory_space=pltpu.SMEM)
    flat = pl.pallas_call(
        functools.partial(body, dims),
        out_shape=jax.ShapeDtypeStruct((ROWS, BE * C), BF16),
        in_specs=[vmem, vmem, vmem, smem, vmem, vmem, vmem, vmem],
        out_specs=vmem,
        scratch_shapes=[
            pltpu.VMEM((WIDE, points), BF16),
            pltpu.VMEM((columns * 16, 256), BF16),
            pltpu.VMEM((columns, quarter + 16, WIDE), BF16),
            pltpu.VMEM((columns, quarter + 16, WIDE), BF16),
            pltpu.VMEM((ZG * ROWS, WIDE), F32),
            pltpu.VMEM((ROWS, BE), F32),
            pltpu.VMEM((ROWS, BE * C), F32),
            pltpu.VMEM((ROWS, BE * C), BF16),
            pltpu.VMEM((2, 3, (BE + 2) * BE, ZPAD), BF16),
            pltpu.VMEM((9 * TAP, WIDE), BF16),
            pltpu.VMEM((9 * TAP, WIDE), BF16),
            pltpu.VMEM((4, BE, BE * C), BF16),
            pltpu.VMEM((4, BE, BE * C), BF16),
            pltpu.SemaphoreType.DMA((columns,)),
            pltpu.SemaphoreType.DMA((columns,)),
            pltpu.SemaphoreType.DMA((4,)),
            pltpu.SemaphoreType.DMA((4,)),
        ],
        compiler_params=pltpu.CompilerParams(
            collective_id=0, has_side_effects=True, vmem_limit_bytes=56 * 2**20
        ),
    )(
        point_feats.T,
        point_block.T,
        point_voxel.reshape(1, points),
        neighbours,
        conv_one,
        bias_one.reshape(1, C),
        conv_two,
        bias_two.reshape(1, C),
    )
    return flat.reshape(1, BE, BE, BE, C)


def solution(mesh):
    dims = (mesh.shape["region"], mesh.shape["block"])
    return jax.shard_map(
        functools.partial(per_device, dims),
        mesh=mesh,
        in_specs=(
            P(("region", "block"), None),
            P(("region", "block"), None),
            P(("region", "block")),
            P(("region", "block"), None),
            P(),
            P(),
            P(),
            P(),
        ),
        out_specs=P(("region", "block"), None, None, None, None),
        check_vma=False,
    )
```

profile of v0, /device:TPU:1, one launch (start us, length us, event | category | flops | bytes accessed | tf_op | source)
XLA Modules:
  0.0 39.4 jit_solution(1571830545749268507)
XLA Ops:
  0.0 36.9 %shard_map.82 = bf16[256,1024]{1,0:T(8,128)(2,1)} custom-call(bf16[64,3072]{1,0:T(8,128)(2,1)} %bitcast.5, s32[1,3072]{1,0:T(1,128)} %bitcast.6, s32[1,3072]{1,0:T(1,128)} %bitcast.7, s32[1,6]{1,0:T(1,128)} %link_ref.1, bf16[27,64,64]{2,1,0:T(8,128)(2,1)} %one_ref.1, f32[1,64]{1,0:T(1,128)} %bitcast.8, bf16[27,64,64]{2,1,0:T(8,128)(2,1)} %two_ref.1, ...), custom_call_target="tpu_custom_call" | custom-call | tf_op jit(solution)/shard_map/pallas_call | solution.py:417
  36.9 2.5 %reshape.15 = bf16[1,16,16,16,64]{4,3,2,1,0:T(8,128)(2,1)} reshape(bf16[256,1024]{1,0:T(8,128)(2,1)} %shard_map.82) | data formatting | bytes 1048576 | tf_op jit(solution)/shard_map/reshape | solution.py:454
where the time goes:
time: 39.5 us; the launch traced here: 39.4 us
  Pallas kernels  36.9 us (93%)
  local copies, waits for them, and re-layouts  2.48 us (6%)
    pallas_call x1, Pallas kernels, per_device(): pl.pallas_call(functools.partial(body, dims), out_shape=jax.ShapeDtypeStr...  36.9 us
    reshape x1, local copies, waits for them, and re-layouts, per_device(): return flat.reshape(1, BE, BE, BE, C)  2.48 us

commit v1 on v0

--- a/solution.py
+++ b/solution.py
@@ -12,6 +12,9 @@
 C = 64
 ROWS = BE * BE
 ZG = 4
+BATCH = 4
+PARTS = 8
+UNROLL = 16
 WIDE = 4 * C
 ZPAD = (BE + 2) * C
 TAP = 6 * C
@@ -89,32 +92,30 @@
     field_ref[2, rows, :] = up.astype(BF16)
 
 
-def convolve(field_ref, wide_ref, plane, count):
+def convolve(field_ref, wide_ref, runs):
     def window(tap, group):
         dx, dy = divmod(tap, 3)
-        start = (plane + dx) * BE
-        return field_ref[dy, start : start + count * BE, group * WIDE : group * WIDE + TAP]
+        cols = slice(group * WIDE, group * WIDE + TAP)
+        return [field_ref[dy, (p + dx) * BE : (p + dx + n) * BE, cols] for p, n in runs]
 
     total = None
     for first in range(0, 9, 2):
         taps = [t for t in (first, first + 1) if t < 9]
-        left = jnp.concatenate(
-            [
-                jnp.concatenate([window(t, group) for t in taps], axis=1)
-                for group in range(ZG)
-            ],
-            axis=0,
-        )
+        columns = [
+            jnp.concatenate([part for group in range(ZG) for part in window(t, group)], axis=0)
+            for t in taps
+        ]
         right = wide_ref[first * TAP : (first + len(taps)) * TAP, :]
-        part = jnp.dot(left, right, preferred_element_type=F32)
+        part = jnp.dot(jnp.concatenate(columns, axis=1), right, preferred_element_type=F32)
         total = part if total is None else total + part
     return total
 
 
 def body(
-    dims, feats_ref, blk_ref, vox_ref, link_ref, one_ref, bone_ref, two_ref, btwo_ref, out_ref,
-    expanded, indices, send, recv, sums, counts, inverse, voxels, field, wide_one, wide_two,
-    side_out, side_in, send_sem, recv_sem, side_send, side_recv,
+    dims, feats_hbm, blk_ref, vox_hbm, link_ref, one_hbm, bone_ref, two_hbm, btwo_ref, out_ref,
+    feats_ref, vox_ref, one_ref, two_ref,
+    expanded, indices, send, recv, sums, counts, inverse, voxels, hidden, field, wide_one, wide_two,
+    side_out, side_in, send_sem, recv_sem, side_send, side_recv, load_sem,
 ):
     regions, columns = dims
     side = math.isqrt(columns)
@@ -123,6 +124,14 @@
     quarter = cap // 4
     region, block = lax.axis_index("region"), lax.axis_index("block")
     my_y, my_x = block // side, block % side
+    loads = [
+        pltpu.make_async_copy(source, target, load_sem.at[k])
+        for k, (source, target) in enumerate(
+            [(vox_hbm, vox_ref), (feats_hbm, feats_ref), (one_hbm, one_ref), (two_hbm, two_ref)]
+        )
+    ]
+    for load in loads:
+        load.start()
 
     def at(dy, dx):
         return lax.rem(my_y + dy, side) * side + lax.rem(my_x + dx, side)
@@ -151,6 +160,8 @@
         + (rank >= 3 * quarter).astype(F32)
     )
     high = rank - quarter * low
+    loads[0].wait()
+    loads[1].wait()
     feats = feats_ref[...]
     for k in range(4):
         expanded[k * C : (k + 1) * C, :] = feats * (low == k).astype(F32).astype(BF16)
@@ -160,11 +171,14 @@
     number = vox_ref[...]
     code_a = (number // 64 + 1).astype(F32).astype(BF16)
     code_b = (number % 64).astype(F32).astype(BF16)
-    slot_row = (blk.astype(F32) * 16 + third).astype(BF16)
-    where_to = onehot(iota((columns * 16, points), 0).astype(F32).astype(BF16), slot_row)
+    slot_row = (blk.astype(F32) * 8 + third).astype(BF16)
+    where_to = onehot(iota((columns * 8, points), 0).astype(F32).astype(BF16), slot_row)
     spots = onehot(iota((128, points), 0).astype(F32).astype(BF16), place)
     codes = jnp.concatenate([spots * code_a, spots * code_b], axis=0)
-    indices[...] = lax.dot_general(where_to, codes, NT, preferred_element_type=F32).astype(BF16)
+    coded = lax.dot_general(where_to, codes, NT, preferred_element_type=F32)
+    for k in range(columns):
+        pair = [coded[k * 8 : (k + 1) * 8, half * 128 : (half + 1) * 128] for half in range(2)]
+        indices[k * 16 : (k + 1) * 16, :] = jnp.concatenate(pair, axis=0).astype(BF16)
 
     arrivals = columns - 1 + (region > 0).astype(jnp.int32) + (region < regions - 1).astype(jnp.int32)
     pl.semaphore_wait(barrier, arrivals)
@@ -200,18 +214,18 @@
             mine = packed[j * quarter : (j + 1) * quarter]
             codes_here = indices[pl.ds(pl.multiple_of(target * 16, 16), 16), :]
 
+            def fill(pack):
+                pack[slot, 0:quarter, :] = mine[:, 0:128]
+                pack[slot, quarter : 2 * quarter, :] = mine[:, 128:256]
+                pack[slot, 2 * quarter : 2 * quarter + 16, :] = codes_here
+
             def ship():
-                send[slot, 0:quarter, :] = mine
-                send[slot, quarter : quarter + 16, :] = codes_here
+                fill(send)
                 copy_to(slot, target).start()
 
             if j == 0:
 
-                @pl.when(turn == 0)
-                def _():
-                    recv[0, 0:quarter, :] = mine
-                    recv[0, quarter : quarter + 16, :] = codes_here
-
+                pl.when(turn == 0)(lambda: fill(recv))
                 pl.when(turn != 0)(ship)
             else:
                 ship()
@@ -219,28 +233,29 @@
 
     lax.fori_loop(0, side, send_group, 0)
 
+    loads[2].wait()
     build_weights(one_ref, wide_one)
+    loads[3].wait()
     build_weights(two_ref, wide_two)
 
     sums[...] = jnp.zeros_like(sums)
     counts[...] = jnp.zeros_like(counts)
 
     def bin_group(step, carry):
-        turn = lax.rem(step + 1, side)
         hots, masked, flat_hots, depth_hots = [], [], [], []
-        for j in range(side):
-            slot = turn * side + j
+        for j in range(BATCH):
+            turn = step * BATCH + j
+            slot = jnp.where(turn == 0, 0, lax.rem(turn + side - 2, columns - 1) + 1)
             if j == 0:
                 pl.when(turn != 0)(lambda: copy_to(slot, block).wait_recv())
             else:
                 copy_to(slot, block).wait_recv()
-            code = recv[slot, quarter : quarter + 16, :].astype(F32)[0:8]
-            a = code[:, 0:128].astype(jnp.int32) - 1
-            b = code[:, 128:256].astype(jnp.int32)
+            code = recv[slot, 2 * quarter : 2 * quarter + 16, :].astype(F32)
+            a = code[0:8].astype(jnp.int32) - 1
+            b = code[8:16].astype(jnp.int32)
             flat = a * 4 + (b >> 4)
             deep = (b >> 2) & 3
             inner = (b & 3).astype(F32)
-            level = jnp.where(a >= 0, b & 15, -1).astype(F32)
             flat = flat.astype(F32)
             pieces = cap // 128
             ids = iota((ROWS, 128), 0).astype(F32).astype(BF16)
@@ -253,16 +268,13 @@
                     )
                 )
             hots.append(jnp.concatenate(by_group, axis=0))
-            flat_hots.append(
-                jnp.concatenate(
-                    [onehot(ids, flat[k : k + 1].astype(BF16)) for k in range(pieces)], axis=1
+            coarse, fine = a.astype(F32), b.astype(F32)
+            for hot_list, value in ((flat_hots, coarse), (depth_hots, fine)):
+                hot_list.append(
+                    jnp.concatenate(
+                        [onehot(ids[:64], value[k : k + 1].astype(BF16)) for k in range(pieces)], axis=1
+                    )
                 )
-            )
-            depth_hots.append(
-                jnp.concatenate(
-                    [onehot(ids[:BE], level[k : k + 1].astype(BF16)) for k in range(pieces)], axis=1
-                )
-            )
             turned = inner.T
             of_lane = (iota((128, WIDE), 1) // C).astype(F32)
             choose = jnp.concatenate(
@@ -270,7 +282,8 @@
             ).astype(BF16)
             quads = []
             for k in range(4):
-                piece = recv[slot, 0:quarter, k * C : (k + 1) * C]
+                start, col = k // 2 * quarter, k % 2 * C
+                piece = recv[slot, start : start + quarter, col : col + C]
                 quads.append(jnp.concatenate([piece] * 4, axis=1))
             masked.append(jnp.concatenate(quads, axis=0) * choose)
         hot = jnp.concatenate(hots, axis=1)
@@ -283,9 +296,9 @@
         )
         return carry
 
-    lax.fori_loop(0, side, bin_group, 0)
-
-    tally = counts[...]
+    lax.fori_loop(0, columns // BATCH, bin_group, 0)
+
+    tally = pltpu.einshape("a(bc)->(ab)c", counts[...], b=ZG)
     share = jnp.where(tally > 0.5, 1.0 / jnp.maximum(tally, 1.0), 0.0)
     first = share.astype(BF16)
     rest = share - first.astype(F32)
@@ -342,10 +355,10 @@
         pl.when(region < regions - 1)(lambda: side_copy(layer, 1).wait_send())
 
     def mean_plane(x):
-        rows = pl.ds(pl.multiple_of(x * BE, BE), BE)
+        rows = slice(x * BE, (x + 1) * BE)
         groups = []
         for z in range(ZG):
-            total = sums[pl.ds(pl.multiple_of(z * ROWS + x * BE, BE), BE), :]
+            total = sums[z * ROWS + x * BE : z * ROWS + (x + 1) * BE, :]
             mean = (total * inverse[rows, z * WIDE : (z + 1) * WIDE]).astype(BF16)
             voxels[rows, z * WIDE : (z + 1) * WIDE] = mean
             groups.append(mean.astype(F32))
@@ -356,46 +369,42 @@
     side_out[0] = voxels[0:BE, :]
     side_out[1] = voxels[ROWS - BE : ROWS, :]
     send_sides(0)
-    lax.fori_loop(1, BE - 1, lambda x, carry: (mean_plane(x), carry)[1], 0)
-
-    def encode(layer, plane, count, bias, save):
-        total = convolve(field.at[layer], wide_one if layer == 0 else wide_two, plane, count)
-        for x in range(count):
-            rows = slice((plane + x) * BE, (plane + x + 1) * BE)
-            groups = []
-            for z in range(ZG):
-                cols = slice(z * WIDE, (z + 1) * WIDE)
-                start = z * count * BE + x * BE
-                value = total[start : start + BE] + bias
+    for x in range(1, BE - 1):
+        mean_plane(x)
+
+    def encode(layer, runs, bias, target):
+        total = convolve(field.at[layer], wide_two if layer else wide_one, runs)
+        start = 0
+        for group in range(ZG):
+            cols = slice(group * WIDE, (group + 1) * WIDE)
+            for p, n in runs:
+                rows = slice(p * BE, (p + n) * BE)
+                value = total[start : start + n * BE] + bias
+                start += n * BE
                 if layer:
                     value = value + voxels[rows, cols].astype(F32)
                 value = jnp.where(inverse[rows, cols] > 0.0, jnp.maximum(value, 0.0), 0.0)
-                groups.append(value)
-            save(plane + x, groups)
+                target[rows, cols] = value.astype(BF16)
+
+    def place_hidden(x):
+        rows = pl.ds(pl.multiple_of(x * BE, BE), BE)
+        groups = [hidden[rows, z * WIDE : (z + 1) * WIDE].astype(F32) for z in range(ZG)]
+        place_plane(field.at[1], x + 1, groups, keep_y, keep_z)
 
     bias_one = jnp.concatenate([bone_ref[...]] * 4, axis=1)
     bias_two = jnp.concatenate([btwo_ref[...]] * 4, axis=1)
 
-    def save_hidden(x, groups):
-        groups = [g.astype(BF16) for g in groups]
-        if x in (0, BE - 1):
-            for z in range(ZG):
-                side_out[2 if x == 0 else 3, :, z * WIDE : (z + 1) * WIDE] = groups[z]
-        place_plane(field.at[1], x + 1, [g.astype(F32) for g in groups], keep_y, keep_z)
-
-    def save_out(x, groups):
-        for z in range(ZG):
-            out_ref[x * BE : (x + 1) * BE, z * WIDE : (z + 1) * WIDE] = groups[z].astype(BF16)
-
-    encode(0, 1, BE - 2, bias_one, save_hidden)
+    middle, ends = [(1, BE - 2)], [(0, 1), (BE - 1, 1)]
+    encode(0, middle, bias_one, hidden)
     receive_sides(0)
-    encode(0, 0, 1, bias_one, save_hidden)
-    encode(0, BE - 1, 1, bias_one, save_hidden)
+    encode(0, ends, bias_one, hidden)
+    side_out[2] = hidden[0:BE, :]
+    side_out[3] = hidden[ROWS - BE : ROWS, :]
     send_sides(1)
-    encode(1, 1, BE - 2, bias_two, save_out)
+    lax.fori_loop(0, BE, lambda x, carry: (place_hidden(x), carry)[1], 0, unroll=UNROLL)
+    encode(1, middle, bias_two, out_ref)
     receive_sides(1)
-    encode(1, 0, 1, bias_two, save_out)
-    encode(1, BE - 1, 1, bias_two, save_out)
+    encode(1, ends, bias_two, out_ref)
 
     def settle(slot, carry):
         copy_to(slot, block).wait_send()
@@ -404,6 +413,18 @@
     lax.fori_loop(1, columns, settle, 0)
     settle_sides(0)
     settle_sides(1)
+
+
+def unfold(flat_ref, out_hbm, tiles, sems):
+    copies = []
+    step = ROWS // PARTS
+    for k in range(PARTS):
+        rows = slice(k * step, (k + 1) * step)
+        tiles[rows] = pltpu.einshape("a(bc)->abc", flat_ref[rows, :], b=BE)
+        copies.append(pltpu.make_async_copy(tiles.at[rows], out_hbm.at[rows], sems.at[k]))
+        copies[-1].start()
+    for copy in copies:
+        copy.wait()
 
 
 def per_device(
@@ -414,19 +435,26 @@
     quarter = 2 * points // columns // 4
     vmem = pl.BlockSpec(memory_space=pltpu.VMEM)
     smem = pl.BlockSpec(memory_space=pltpu.SMEM)
+    hbm = pl.BlockSpec(memory_space=pl.ANY)
+    pack = pltpu.VMEM((columns, 2 * quarter + 16, 128), BF16)
     flat = pl.pallas_call(
         functools.partial(body, dims),
         out_shape=jax.ShapeDtypeStruct((ROWS, BE * C), BF16),
-        in_specs=[vmem, vmem, vmem, smem, vmem, vmem, vmem, vmem],
+        in_specs=[hbm, vmem, hbm, smem, hbm, vmem, hbm, vmem],
         out_specs=vmem,
         scratch_shapes=[
+            pltpu.VMEM((C, points), BF16),
+            pltpu.VMEM((1, points), jnp.int32),
+            pltpu.VMEM((27, C, C), BF16),
+            pltpu.VMEM((27, C, C), BF16),
             pltpu.VMEM((WIDE, points), BF16),
-            pltpu.VMEM((columns * 16, 256), BF16),
-            pltpu.VMEM((columns, quarter + 16, WIDE), BF16),
-            pltpu.VMEM((columns, quarter + 16, WIDE), BF16),
+            pltpu.VMEM((columns * 16, 128), BF16),
+            pack,
+            pack,
             pltpu.VMEM((ZG * ROWS, WIDE), F32),
-            pltpu.VMEM((ROWS, BE), F32),
+            pltpu.VMEM((64, 64), F32),
             pltpu.VMEM((ROWS, BE * C), F32),
+            pltpu.VMEM((ROWS, BE * C), BF16),
             pltpu.VMEM((ROWS, BE * C), BF16),
             pltpu.VMEM((2, 3, (BE + 2) * BE, ZPAD), BF16),
             pltpu.VMEM((9 * TAP, WIDE), BF16),
@@ -437,9 +465,10 @@
             pltpu.SemaphoreType.DMA((columns,)),
             pltpu.SemaphoreType.DMA((4,)),
             pltpu.SemaphoreType.DMA((4,)),
+            pltpu.SemaphoreType.DMA((4,)),
         ],
         compiler_params=pltpu.CompilerParams(
-            collective_id=0, has_side_effects=True, vmem_limit_bytes=56 * 2**20
+            collective_id=0, has_side_effects=True, vmem_limit_bytes=60 * 2**20
         ),
     )(
         point_feats.T,
@@ -451,7 +480,15 @@
         conv_two,
         bias_two.reshape(1, C),
     )
-    return flat.reshape(1, BE, BE, BE, C)
+    out = pl.pallas_call(
+        unfold,
+        out_shape=jax.ShapeDtypeStruct((ROWS, BE, C), BF16),
+        in_specs=[vmem],
+        out_specs=hbm,
+        scratch_shapes=[pltpu.VMEM((ROWS, BE, C), BF16), pltpu.SemaphoreType.DMA((PARTS,))],
+        compiler_params=pltpu.CompilerParams(vmem_limit_bytes=8 * 2**20),
+    )(flat)
+    return out.reshape(1, BE, BE, BE, C)
 
 
 def solution(mesh):

time: 39.5 us -> 35.2 us (0.89)
  Pallas kernels: 36.9 us -> 33.9 us
  local copies, waits for them, and re-layouts: 2.48 us -> 1.03 us
    pallas_call x1, Pallas kernels: 36.9 us -> 32.8 us  [per_device(): pl.pallas_call(functools.partial(body, dims), out_shape=jax.ShapeDtypeStr...]
    reshape x1 -> x0, local copies, waits for them, and re-layouts: 2.48 us -> none  [per_device(): return flat.reshape(1, BE, BE, BE, C)]
    pallas_call x0 -> x1, Pallas kernels: none -> 1.14 us  [per_device(): pl.pallas_call(unfold, out_shape=jax.ShapeDtypeStruct((ROWS, BE, C), BF16...]
    unnamed x0 -> x2, local copies, waits for them, and re-layouts: none -> 1.03 us
where the time goes in v1:
time: 35.2 us; the launch traced here: 35 us
  Pallas kernels  33.9 us (96%)
  local copies, waits for them, and re-layouts  1.03 us (3%)
    pallas_call x1, Pallas kernels, per_device(): pl.pallas_call(functools.partial(body, dims), out_shape=jax.ShapeDtypeStr...  32.8 us
    pallas_call x1, Pallas kernels, per_device(): pl.pallas_call(unfold, out_shape=jax.ShapeDtypeStruct((ROWS, BE, C), BF16...  1.14 us
    unnamed x2, local copies, waits for them, and re-layouts  1.03 us

profile of v1, /device:TPU:1, one launch (start us, length us, event | category | flops | bytes accessed | tf_op | source)
XLA Modules:
  0.0 35.0 jit_solution(13723844387605527958)
XLA Ops:
  0.0 32.8 %shard_map.82.flat_ref = bf16[256,1024]{1,0:T(8,128)(2,1)} custom-call(bf16[64,3072]{1,0:T(8,128)(2,1)} %bitcast.6, s32[1,3072]{1,0:T(1,128)} %bitcast.7, s32[1,3072]{1,0:T(1,128)} %bitcast.8, s32[1,6]{1,0:T(1,128)} %link_ref.1, bf16[27,64,64]{2,1,0:T(8,128)(2,1)} %one_hbm.1, f32[1,64]{1,0:T(1,128)} %bitcast.9, bf16[27,64,64]{2,1,0:T(8,128)(2,1)} %two_hbm.1, ...), custom_call_target="tpu_custom_call" | custom-call | tf_op jit(solution)/shard_map/pallas_call | solution.py:440
  32.8 0.0 copy-start
  32.8 1.0 %copy-done = bf16[256,1024]{1,0:T(8,128)(2,1)S(1)} copy-done((bf16[256,1024]{1,0:T(8,128)(2,1)S(1)}, bf16[256,1024]{1,0:T(8,128)(2,1)}, u32[]{:S(2)}) %copy-start) | copy-done | bytes 524312
  33.8 1.1 %shard_map.83 = bf16[256,16,64]{2,1,0:T(8,128)(2,1)} custom-call(bf16[256,1024]{1,0:T(8,128)(2,1)S(1)} %copy-done), custom_call_target="tpu_custom_call" | custom-call | tf_op jit(solution)/shard_map/pallas_call | solution.py:483
Async XLA Ops:
  32.8 1.0 %copy-start = (bf16[256,1024]{1,0:T(8,128)(2,1)S(1)}, bf16[256,1024]{1,0:T(8,128)(2,1)}, u32[]{:S(2)}) copy-start(bf16[256,1024]{1,0:T(8,128)(2,1)} %shard_map.82.flat_ref) | copy-start | bytes 1572868

commit v2 on v1

--- a/solution.py
+++ b/solution.py
@@ -114,8 +114,8 @@
 def body(
     dims, feats_hbm, blk_ref, vox_hbm, link_ref, one_hbm, bone_ref, two_hbm, btwo_ref, out_ref,
     feats_ref, vox_ref, one_ref, two_ref,
-    expanded, indices, send, recv, sums, counts, inverse, voxels, hidden, field, wide_one, wide_two,
-    side_out, side_in, send_sem, recv_sem, side_send, side_recv, load_sem,
+    expanded, indices, codes_in, send, recv, sums, counts, inverse, voxels, hidden, field, wide_one, wide_two,
+    side_out, side_in, send_sem, recv_sem, side_send, side_recv, load_sem, code_send, code_recv,
 ):
     regions, columns = dims
     side = math.isqrt(columns)
@@ -192,6 +192,26 @@
             device_id=(region, target),
             device_id_type=MESH,
         )
+
+    def code_copy(slot, target):
+        rows = pl.ds(pl.multiple_of(target * 16, 16), 16)
+        return pltpu.make_async_remote_copy(
+            src_ref=indices.at[rows],
+            dst_ref=codes_in.at[slot],
+            send_sem=code_send.at[slot],
+            recv_sem=code_recv.at[slot],
+            device_id=(region, target),
+            device_id_type=MESH,
+        )
+
+    def send_codes(slot, carry):
+        j = lax.rem(slot, side)
+        code_copy(slot, at(j, lax.rem(slot // side + j, side))).start()
+        return carry
+
+    lax.fori_loop(side, columns, send_codes, 0)
+    lax.fori_loop(1, side, send_codes, 0)
+    codes_in[0] = indices[pl.ds(pl.multiple_of(block * 16, 16), 16), :]
 
     def send_group(step, carry):
         turn = lax.rem(step + 1, side)
@@ -212,12 +232,10 @@
         for j, target in enumerate(targets):
             slot = turn * side + j
             mine = packed[j * quarter : (j + 1) * quarter]
-            codes_here = indices[pl.ds(pl.multiple_of(target * 16, 16), 16), :]
 
             def fill(pack):
                 pack[slot, 0:quarter, :] = mine[:, 0:128]
                 pack[slot, quarter : 2 * quarter, :] = mine[:, 128:256]
-                pack[slot, 2 * quarter : 2 * quarter + 16, :] = codes_here
 
             def ship():
                 fill(send)
@@ -241,40 +259,68 @@
     sums[...] = jnp.zeros_like(sums)
     counts[...] = jnp.zeros_like(counts)
 
-    def bin_group(step, carry):
-        hots, masked, flat_hots, depth_hots = [], [], [], []
+    pieces = cap // 128
+    names = iota((ROWS, 128), 0).astype(F32).astype(BF16)
+
+    def slot_at(turn):
+        return jnp.where(turn == 0, 0, lax.rem(turn + side - 2, columns - 1) + 1)
+
+    def arrive(copy, turn, first):
+        if first:
+            pl.when(turn != 0)(lambda: copy(slot_at(turn), block).wait_recv())
+        else:
+            copy(slot_at(turn), block).wait_recv()
+
+    def count_group(step, carry):
+        tables = ([], [])
         for j in range(BATCH):
             turn = step * BATCH + j
-            slot = jnp.where(turn == 0, 0, lax.rem(turn + side - 2, columns - 1) + 1)
-            if j == 0:
-                pl.when(turn != 0)(lambda: copy_to(slot, block).wait_recv())
-            else:
-                copy_to(slot, block).wait_recv()
-            code = recv[slot, 2 * quarter : 2 * quarter + 16, :].astype(F32)
+            arrive(code_copy, turn, j == 0)
+            code = codes_in[slot_at(turn)].astype(F32)
+            for table, value in zip(tables, (code[0:8] - 1.0, code[8:16])):
+                for k in range(pieces):
+                    table.append(onehot(names[:64], value[k : k + 1].astype(BF16)))
+        coarse, fine = [jnp.concatenate(table, axis=1) for table in tables]
+        counts[...] += lax.dot_general(coarse, fine, NT, preferred_element_type=F32)
+        return carry
+
+    lax.fori_loop(0, columns // BATCH, count_group, 0)
+    tally = pltpu.einshape("a(bc)->(ab)c", counts[...], b=ZG)
+    share = jnp.where(tally > 0.5, 1.0 / jnp.maximum(tally, 1.0), 0.0)
+    first = share.astype(BF16)
+    rest = share - first.astype(F32)
+    second = rest.astype(BF16)
+    third_part = (rest - second.astype(F32)).astype(BF16)
+    spread = jnp.where(iota((BE, BE * C), 0) == iota((BE, BE * C), 1) // C, 1.0, 0.0).astype(BF16)
+    inverse[...] = (
+        jnp.dot(first, spread, preferred_element_type=F32)
+        + jnp.dot(second, spread, preferred_element_type=F32)
+        + jnp.dot(third_part, spread, preferred_element_type=F32)
+    )
+
+
+    def bin_group(base, size):
+        hots, masked = [], []
+        for j in range(size):
+            turn = base + j
+            slot = slot_at(turn)
+            arrive(copy_to, turn, j == 0)
+            code = codes_in[slot].astype(F32)
             a = code[0:8].astype(jnp.int32) - 1
             b = code[8:16].astype(jnp.int32)
             flat = a * 4 + (b >> 4)
             deep = (b >> 2) & 3
             inner = (b & 3).astype(F32)
             flat = flat.astype(F32)
-            pieces = cap // 128
-            ids = iota((ROWS, 128), 0).astype(F32).astype(BF16)
             by_group = []
             for group in range(ZG):
                 row = jnp.where(deep == group, flat, -1.0)
                 by_group.append(
                     jnp.concatenate(
-                        [onehot(ids, row[k : k + 1].astype(BF16)) for k in range(pieces)], axis=1
+                        [onehot(names, row[k : k + 1].astype(BF16)) for k in range(pieces)], axis=1
                     )
                 )
             hots.append(jnp.concatenate(by_group, axis=0))
-            coarse, fine = a.astype(F32), b.astype(F32)
-            for hot_list, value in ((flat_hots, coarse), (depth_hots, fine)):
-                hot_list.append(
-                    jnp.concatenate(
-                        [onehot(ids[:64], value[k : k + 1].astype(BF16)) for k in range(pieces)], axis=1
-                    )
-                )
             turned = inner.T
             of_lane = (iota((128, WIDE), 1) // C).astype(F32)
             choose = jnp.concatenate(
@@ -288,27 +334,9 @@
             masked.append(jnp.concatenate(quads, axis=0) * choose)
         hot = jnp.concatenate(hots, axis=1)
         sums[...] += jnp.dot(hot, jnp.concatenate(masked, axis=0), preferred_element_type=F32)
-        counts[...] += lax.dot_general(
-            jnp.concatenate(flat_hots, axis=1),
-            jnp.concatenate(depth_hots, axis=1),
-            NT,
-            preferred_element_type=F32,
-        )
-        return carry
-
-    lax.fori_loop(0, columns // BATCH, bin_group, 0)
-
-    tally = pltpu.einshape("a(bc)->(ab)c", counts[...], b=ZG)
-    share = jnp.where(tally > 0.5, 1.0 / jnp.maximum(tally, 1.0), 0.0)
-    first = share.astype(BF16)
-    rest = share - first.astype(F32)
-    second = rest.astype(BF16)
-    third_part = (rest - second.astype(F32)).astype(BF16)
-    spread = jnp.where(iota((BE, BE * C), 0) == iota((BE, BE * C), 1) // C, 1.0, 0.0).astype(BF16)
-    inverse[...] = (
-        jnp.dot(first, spread, preferred_element_type=F32)
-        + jnp.dot(second, spread, preferred_element_type=F32)
-        + jnp.dot(third_part, spread, preferred_element_type=F32)
+
+    lax.fori_loop(
+        0, columns // BATCH, lambda step, carry: (bin_group(step * BATCH, BATCH), carry)[1], 0
     )
 
     keep_y = (link_ref[0, 2] >= 0).astype(F32)
@@ -408,6 +436,7 @@
 
     def settle(slot, carry):
         copy_to(slot, block).wait_send()
+        code_copy(slot, block).wait_send()
         return carry
 
     lax.fori_loop(1, columns, settle, 0)
@@ -436,7 +465,7 @@
     vmem = pl.BlockSpec(memory_space=pltpu.VMEM)
     smem = pl.BlockSpec(memory_space=pltpu.SMEM)
     hbm = pl.BlockSpec(memory_space=pl.ANY)
-    pack = pltpu.VMEM((columns, 2 * quarter + 16, 128), BF16)
+    pack = pltpu.VMEM((columns, 2 * quarter, 128), BF16)
     flat = pl.pallas_call(
         functools.partial(body, dims),
         out_shape=jax.ShapeDtypeStruct((ROWS, BE * C), BF16),
@@ -449,6 +478,7 @@
             pltpu.VMEM((27, C, C), BF16),
             pltpu.VMEM((WIDE, points), BF16),
             pltpu.VMEM((columns * 16, 128), BF16),
+            pltpu.VMEM((columns, 16, 128), BF16),
             pack,
             pack,
             pltpu.VMEM((ZG * ROWS, WIDE), F32),
@@ -466,6 +496,8 @@
             pltpu.SemaphoreType.DMA((4,)),
             pltpu.SemaphoreType.DMA((4,)),
             pltpu.SemaphoreType.DMA((4,)),
+            pltpu.SemaphoreType.DMA((columns,)),
+            pltpu.SemaphoreType.DMA((columns,)),
         ],
         compiler_params=pltpu.CompilerParams(
             collective_id=0, has_side_effects=True, vmem_limit_bytes=60 * 2**20

time: 35.2 us -> 34.9 us (level)
  no operation moved by 1% of the time
where the time goes in v2:
time: 34.9 us; the launch traced here: 34.7 us
  Pallas kernels  33.6 us (96%)
  local copies, waits for them, and re-layouts  1.03 us (3%)
    pallas_call x1, Pallas kernels, per_device(): pl.pallas_call(functools.partial(body, dims), out_shape=jax.ShapeDtypeStr...  32.5 us
    pallas_call x1, Pallas kernels, per_device(): pl.pallas_call(unfold, out_shape=jax.ShapeDtypeStruct((ROWS, BE, C), BF16...  1.14 us
    unnamed x2, local copies, waits for them, and re-layouts  1.03 us

profile of v2, /device:TPU:1, one launch (start us, length us, event | category | flops | bytes accessed | tf_op | source)
XLA Modules:
  0.0 34.7 jit_solution(316680733717263891)
XLA Ops:
  0.0 32.5 %shard_map.82.flat_ref = bf16[256,1024]{1,0:T(8,128)(2,1)} custom-call(bf16[64,3072]{1,0:T(8,128)(2,1)} %bitcast.6, s32[1,3072]{1,0:T(1,128)} %bitcast.7, s32[1,3072]{1,0:T(1,128)} %bitcast.8, s32[1,6]{1,0:T(1,128)} %link_ref.1, bf16[27,64,64]{2,1,0:T(8,128)(2,1)} %one_hbm.1, f32[1,64]{1,0:T(1,128)} %bitcast.9, bf16[27,64,64]{2,1,0:T(8,128)(2,1)} %two_hbm.1, ...), custom_call_target="tpu_custom_call" | custom-call | tf_op jit(solution)/shard_map/pallas_call | solution.py:469
  32.5 0.0 copy-start
  32.5 1.0 %copy-done = bf16[256,1024]{1,0:T(8,128)(2,1)S(1)} copy-done((bf16[256,1024]{1,0:T(8,128)(2,1)S(1)}, bf16[256,1024]{1,0:T(8,128)(2,1)}, u32[]{:S(2)}) %copy-start) | copy-done | bytes 524312
  33.5 1.1 %shard_map.83 = bf16[256,16,64]{2,1,0:T(8,128)(2,1)} custom-call(bf16[256,1024]{1,0:T(8,128)(2,1)S(1)} %copy-done), custom_call_target="tpu_custom_call" | custom-call | tf_op jit(solution)/shard_map/pallas_call | solution.py:515
Async XLA Ops:
  32.5 1.0 %copy-start = (bf16[256,1024]{1,0:T(8,128)(2,1)S(1)}, bf16[256,1024]{1,0:T(8,128)(2,1)}, u32[]{:S(2)}) copy-start(bf16[256,1024]{1,0:T(8,128)(2,1)} %shard_map.82.flat_ref) | copy-start | bytes 1572868

commit v3 on v2

--- a/solution.py
+++ b/solution.py
@@ -112,10 +112,10 @@
 
 
 def body(
-    dims, feats_hbm, blk_ref, vox_hbm, link_ref, one_hbm, bone_ref, two_hbm, btwo_ref, out_ref,
+    dims, feats_hbm, blk_ref, vox_hbm, link_ref, one_hbm, bone_ref, two_hbm, btwo_ref, out_hbm,
     feats_ref, vox_ref, one_ref, two_ref,
     expanded, indices, codes_in, send, recv, sums, counts, inverse, voxels, hidden, field, wide_one, wide_two,
-    side_out, side_in, send_sem, recv_sem, side_send, side_recv, load_sem, code_send, code_recv,
+    side_out, side_in, send_sem, recv_sem, side_send, side_recv, load_sem, code_send, code_recv, result, save_sem,
 ):
     regions, columns = dims
     side = math.isqrt(columns)
@@ -214,8 +214,9 @@
     codes_in[0] = indices[pl.ds(pl.multiple_of(block * 16, 16), 16), :]
 
     def send_group(step, carry):
-        turn = lax.rem(step + 1, side)
-        targets = [at(j, lax.rem(turn + j, side)) for j in range(side)]
+        turns = [lax.rem(2 * step + 1 + q, side) for q in range(2)]
+        places = [(turn, j) for turn in turns for j in range(side)]
+        targets = [at(j, lax.rem(turn + j, side)) for turn, j in places]
         blocks = blk_ref[...]
         placing = jnp.concatenate(
             [
@@ -229,9 +230,10 @@
         )
         packed = lax.dot_general(placing, expanded[...], NT, preferred_element_type=F32)
         packed = packed.astype(BF16)
-        for j, target in enumerate(targets):
+        for k, target in enumerate(targets):
+            turn, j = places[k]
             slot = turn * side + j
-            mine = packed[j * quarter : (j + 1) * quarter]
+            mine = packed[k * quarter : (k + 1) * quarter]
 
             def fill(pack):
                 pack[slot, 0:quarter, :] = mine[:, 0:128]
@@ -249,7 +251,7 @@
                 ship()
         return carry
 
-    lax.fori_loop(0, side, send_group, 0)
+    lax.fori_loop(0, side // 2, send_group, 0)
 
     loads[2].wait()
     build_weights(one_ref, wide_one)
@@ -430,9 +432,17 @@
     side_out[3] = hidden[ROWS - BE : ROWS, :]
     send_sides(1)
     lax.fori_loop(0, BE, lambda x, carry: (place_hidden(x), carry)[1], 0, unroll=UNROLL)
-    encode(1, middle, bias_two, out_ref)
+    spans = [slice(BE, ROWS - BE), slice(0, BE), slice(ROWS - BE, ROWS)]
+    saves = [
+        pltpu.make_async_copy(result.at[rows], out_hbm.at[rows], save_sem.at[k])
+        for k, rows in enumerate(spans)
+    ]
+    encode(1, middle, bias_two, result)
+    saves[0].start()
     receive_sides(1)
-    encode(1, ends, bias_two, out_ref)
+    encode(1, ends, bias_two, result)
+    saves[1].start()
+    saves[2].start()
 
     def settle(slot, carry):
         copy_to(slot, block).wait_send()
@@ -442,6 +452,8 @@
     lax.fori_loop(1, columns, settle, 0)
     settle_sides(0)
     settle_sides(1)
+    for save in saves:
+        save.wait()
 
 
 def unfold(flat_ref, out_hbm, tiles, sems):
@@ -470,7 +482,7 @@
         functools.partial(body, dims),
         out_shape=jax.ShapeDtypeStruct((ROWS, BE * C), BF16),
         in_specs=[hbm, vmem, hbm, smem, hbm, vmem, hbm, vmem],
-        out_specs=vmem,
+        out_specs=hbm,
         scratch_shapes=[
             pltpu.VMEM((C, points), BF16),
             pltpu.VMEM((1, points), jnp.int32),
@@ -498,6 +510,8 @@
             pltpu.SemaphoreType.DMA((4,)),
             pltpu.SemaphoreType.DMA((columns,)),
             pltpu.SemaphoreType.DMA((columns,)),
+            pltpu.VMEM((ROWS, BE * C), BF16),
+            pltpu.SemaphoreType.DMA((3,)),
         ],
         compiler_params=pltpu.CompilerParams(
             collective_id=0, has_side_effects=True, vmem_limit_bytes=60 * 2**20

time: 34.9 us -> 34.4 us (0.986)
  Pallas kernels: 33.6 us -> 33.1 us
    pallas_call x1, Pallas kernels: 32.5 us -> 31.9 us  [per_device(): pl.pallas_call(functools.partial(body, dims), out_shape=jax.ShapeDtypeStr...]
where the time goes in v3:
time: 34.4 us; the launch traced here: 34.1 us
  Pallas kernels  33.1 us (96%)
  local copies, waits for them, and re-layouts  1.03 us (3%)
    pallas_call x1, Pallas kernels, per_device(): pl.pallas_call(functools.partial(body, dims), out_shape=jax.ShapeDtypeStr...  31.9 us
    pallas_call x1, Pallas kernels, per_device(): pl.pallas_call(unfold, out_shape=jax.ShapeDtypeStruct((ROWS, BE, C), BF16...  1.14 us
    unnamed x2, local copies, waits for them, and re-layouts  1.03 us

profile of v3, /device:TPU:1, one launch (start us, length us, event | category | flops | bytes accessed | tf_op | source)
XLA Modules:
  0.0 34.1 jit_solution(13230563765738005612)
XLA Ops:
  0.0 31.9 %shard_map.82.flat_ref = bf16[256,1024]{1,0:T(8,128)(2,1)} custom-call(bf16[64,3072]{1,0:T(8,128)(2,1)} %bitcast.6, s32[1,3072]{1,0:T(1,128)} %bitcast.7, s32[1,3072]{1,0:T(1,128)} %bitcast.8, s32[1,6]{1,0:T(1,128)} %link_ref.1, bf16[27,64,64]{2,1,0:T(8,128)(2,1)} %one_hbm.1, f32[1,64]{1,0:T(1,128)} %bitcast.9, bf16[27,64,64]{2,1,0:T(8,128)(2,1)} %two_hbm.1, ...), custom_call_target="tpu_custom_call" | custom-call | tf_op jit(solution)/shard_map/pallas_call | solution.py:481
  32.0 0.0 copy-start
  32.0 1.0 %copy-done = bf16[256,1024]{1,0:T(8,128)(2,1)S(1)} copy-done((bf16[256,1024]{1,0:T(8,128)(2,1)S(1)}, bf16[256,1024]{1,0:T(8,128)(2,1)}, u32[]{:S(2)}) %copy-start) | copy-done | bytes 524312
  33.0 1.1 %shard_map.83 = bf16[256,16,64]{2,1,0:T(8,128)(2,1)} custom-call(bf16[256,1024]{1,0:T(8,128)(2,1)S(1)} %copy-done), custom_call_target="tpu_custom_call" | custom-call | tf_op jit(solution)/shard_map/pallas_call | solution.py:529
Async XLA Ops:
  32.0 1.0 %copy-start = (bf16[256,1024]{1,0:T(8,128)(2,1)S(1)}, bf16[256,1024]{1,0:T(8,128)(2,1)}, u32[]{:S(2)}) copy-start(bf16[256,1024]{1,0:T(8,128)(2,1)} %shard_map.82.flat_ref) | copy-start | bytes 1572868

commit v4 on v3

--- a/solution.py
+++ b/solution.py
@@ -115,7 +115,7 @@
     dims, feats_hbm, blk_ref, vox_hbm, link_ref, one_hbm, bone_ref, two_hbm, btwo_ref, out_hbm,
     feats_ref, vox_ref, one_ref, two_ref,
     expanded, indices, codes_in, send, recv, sums, counts, inverse, voxels, hidden, field, wide_one, wide_two,
-    side_out, side_in, send_sem, recv_sem, side_send, side_recv, load_sem, code_send, code_recv, result, save_sem,
+    side_in, send_sem, recv_sem, side_send, side_recv, load_sem, code_send, code_recv, result, save_sem,
 ):
     regions, columns = dims
     side = math.isqrt(columns)
@@ -347,7 +347,7 @@
     def side_copy(layer, up):
         k = 2 * layer + up
         return pltpu.make_async_remote_copy(
-            src_ref=side_out.at[k],
+            src_ref=(hidden if layer else voxels).at[pl.ds((ROWS - BE) * up, BE)],
             dst_ref=side_in.at[k],
             send_sem=side_send.at[k],
             recv_sem=side_recv.at[k],
@@ -386,21 +386,24 @@
 
     def mean_plane(x):
         rows = slice(x * BE, (x + 1) * BE)
-        groups = []
         for z in range(ZG):
             total = sums[z * ROWS + x * BE : z * ROWS + (x + 1) * BE, :]
             mean = (total * inverse[rows, z * WIDE : (z + 1) * WIDE]).astype(BF16)
             voxels[rows, z * WIDE : (z + 1) * WIDE] = mean
-            groups.append(mean.astype(F32))
+
+    def place_mean(x):
+        groups = [
+            voxels[x * BE : (x + 1) * BE, z * WIDE : (z + 1) * WIDE].astype(F32) for z in range(ZG)
+        ]
         place_plane(field.at[0], x + 1, groups, keep_y, keep_z)
 
     mean_plane(0)
     mean_plane(BE - 1)
-    side_out[0] = voxels[0:BE, :]
-    side_out[1] = voxels[ROWS - BE : ROWS, :]
     send_sides(0)
     for x in range(1, BE - 1):
         mean_plane(x)
+    for x in range(BE):
+        place_mean(x)
 
     def encode(layer, runs, bias, target):
         total = convolve(field.at[layer], wide_two if layer else wide_one, runs)
@@ -428,8 +431,6 @@
     encode(0, middle, bias_one, hidden)
     receive_sides(0)
     encode(0, ends, bias_one, hidden)
-    side_out[2] = hidden[0:BE, :]
-    side_out[3] = hidden[ROWS - BE : ROWS, :]
     send_sides(1)
     lax.fori_loop(0, BE, lambda x, carry: (place_hidden(x), carry)[1], 0, unroll=UNROLL)
     spans = [slice(BE, ROWS - BE), slice(0, BE), slice(ROWS - BE, ROWS)]
@@ -502,7 +503,6 @@
             pltpu.VMEM((9 * TAP, WIDE), BF16),
             pltpu.VMEM((9 * TAP, WIDE), BF16),
             pltpu.VMEM((4, BE, BE * C), BF16),
-            pltpu.VMEM((4, BE, BE * C), BF16),
             pltpu.SemaphoreType.DMA((columns,)),
             pltpu.SemaphoreType.DMA((columns,)),
             pltpu.SemaphoreType.DMA((4,)),

time: 34.4 us -> 34.3 us (level)
  no operation moved by 1% of the time
where the time goes in v4:
time: 34.3 us; the launch traced here: 34 us
  Pallas kernels  33 us (96%)
  local copies, waits for them, and re-layouts  1.03 us (3%)
    pallas_call x1, Pallas kernels, per_device(): pl.pallas_call(functools.partial(body, dims), out_shape=jax.ShapeDtypeStr...  31.8 us
    pallas_call x1, Pallas kernels, per_device(): pl.pallas_call(unfold, out_shape=jax.ShapeDtypeStruct((ROWS, BE, C), BF16...  1.14 us
    unnamed x2, local copies, waits for them, and re-layouts  1.03 us

profile of v4, /device:TPU:1, one launch (start us, length us, event | category | flops | bytes accessed | tf_op | source)
XLA Modules:
  0.0 34.0 jit_solution(12421137715412959858)
XLA Ops:
  0.0 31.8 %shard_map.82.flat_ref = bf16[256,1024]{1,0:T(8,128)(2,1)} custom-call(bf16[64,3072]{1,0:T(8,128)(2,1)} %bitcast.6, s32[1,3072]{1,0:T(1,128)} %bitcast.7, s32[1,3072]{1,0:T(1,128)} %bitcast.8, s32[1,6]{1,0:T(1,128)} %link_ref.1, bf16[27,64,64]{2,1,0:T(8,128)(2,1)} %one_hbm.1, f32[1,64]{1,0:T(1,128)} %bitcast.9, bf16[27,64,64]{2,1,0:T(8,128)(2,1)} %two_hbm.1, ...), custom_call_target="tpu_custom_call" | custom-call | tf_op jit(solution)/shard_map/pallas_call | solution.py:482
  31.9 0.0 copy-start
  31.9 1.0 %copy-done = bf16[256,1024]{1,0:T(8,128)(2,1)S(1)} copy-done((bf16[256,1024]{1,0:T(8,128)(2,1)S(1)}, bf16[256,1024]{1,0:T(8,128)(2,1)}, u32[]{:S(2)}) %copy-start) | copy-done | bytes 524312
  32.9 1.1 %shard_map.83 = bf16[256,16,64]{2,1,0:T(8,128)(2,1)} custom-call(bf16[256,1024]{1,0:T(8,128)(2,1)S(1)} %copy-done), custom_call_target="tpu_custom_call" | custom-call | tf_op jit(solution)/shard_map/pallas_call | solution.py:529
Async XLA Ops:
  31.9 1.0 %copy-start = (bf16[256,1024]{1,0:T(8,128)(2,1)S(1)}, bf16[256,1024]{1,0:T(8,128)(2,1)}, u32[]{:S(2)}) copy-start(bf16[256,1024]{1,0:T(8,128)(2,1)} %shard_map.82.flat_ref) | copy-start | bytes 1572868
